TPU v7x, 32 devices: a whole 2x2x4 slice. The times are simulated.
32 devices in a mesh: dp: 16 (over z, x, core), shard: 2 (over y).
Axes of the slice: x: 2, y: 2, z: 4, core: 2. Of those that a mesh axis runs over, the one named last changes fastest.
Arguments:
- tokens: bfloat16 [4096, 1024], P(('dp', 'shard')), may hold values from -6 to 6
- cotangent: bfloat16 [4096, 1024], P(('dp', 'shard')), may hold values from -6 to 6
- assign: int32 [4096], P('dp'), may hold values from 0 to 1
- prob: float32 [4096], P('dp'), may hold values from 0.2 to 1
- w_gate: bfloat16 [2, 1024, 4096], P(None, None, 'shard'), may hold values from -0.1875 to 0.1875
- w_up: bfloat16 [2, 1024, 4096], P(None, None, 'shard'), may hold values from -0.1875 to 0.1875
- w_down: bfloat16 [2, 4096, 1024], P(None, 'shard'), may hold values from -0.09375 to 0.09375
Outputs:
- output: bfloat16 [4096, 1024], P(('dp', 'shard'))
- input_grad: bfloat16 [4096, 1024], P(('dp', 'shard'))
- grad_gate: float32 [2, 1024, 4096], P(None, 'dp', 'shard')
- grad_up: float32 [2, 1024, 4096], P(None, 'dp', 'shard')
- grad_down: float32 [2, 4096, 1024], P(None, 'shard', 'dp')
All inputs are finite; a program needn't handle non-finite values.
Results may differ from a plain program's by a relative error of at most 0.0057.
Values may be sent and summed in bfloat16 or wider, within the bound.
A program may use at most 192 MiB of HBM per device.

v0:
```python
import jax
import jax.numpy as jnp
from jax import lax
from jax.sharding import PartitionSpec as P

EXP = 2
BLOCK = 128


def arrange(assign, experts, block_rows):
    row_count = assign.shape[0]
    labels = jnp.arange(experts, dtype=jnp.int32)
    onehot = (assign[:, None] == labels[None, :]).astype(jnp.int32)
    counts = jnp.sum(onehot, axis=0)
    blocks = (counts + block_rows - 1) // block_rows
    block_ends = jnp.cumsum(blocks)
    firsts = block_ends - blocks
    before = jnp.cumsum(onehot, axis=0) - onehot
    rank_in = jnp.sum(onehot * before, axis=1)
    token_slot = jnp.sum(onehot * (firsts * block_rows)[None, :], axis=1) + rank_in
    nblocks = row_count // block_rows + experts - 1
    slot_token = (
        jnp.zeros((nblocks * block_rows,), jnp.int32)
        .at[token_slot]
        .set(jnp.arange(row_count, dtype=jnp.int32))
    )
    slot_live = jnp.zeros((nblocks * block_rows,), jnp.float32).at[token_slot].set(1.0)
    block_index = jnp.arange(nblocks, dtype=jnp.int32)
    block_expert = jnp.minimum(
        jnp.sum((block_ends[None, :] <= block_index[:, None]).astype(jnp.int32), axis=1),
        experts - 1,
    )
    return (token_slot, slot_token, slot_live, block_expert)


def add_at(total, expert, term):
    old = lax.dynamic_index_in_dim(total, expert, 0, keepdims=True)
    return lax.dynamic_update_index_in_dim(total, old + term[None], expert, 0)


def fetch(weights, expert):
    return lax.dynamic_index_in_dim(weights, expert, 0, keepdims=False)


def per_device(tokens, cotangent, assign, prob, w_gate, w_up, w_down):
    width = tokens.shape[1]
    group_tokens, group_grad = (
        lax.all_gather(tokens, "shard", axis=0, tiled=True),
        lax.all_gather(cotangent, "shard", axis=0, tiled=True),
    )
    token_slot, slot_token, slot_live, block_expert = arrange(assign, EXP, BLOCK)
    nblocks = block_expert.shape[0]
    live_rows = slot_live[:, None] > 0
    scaled_grad = (prob[:, None] * group_grad.astype(jnp.float32)).astype(jnp.bfloat16)
    slot_x = jnp.where(
        live_rows, group_tokens[slot_token], jnp.zeros((), group_tokens.dtype)
    ).reshape(nblocks, BLOCK, width)
    slot_dout = jnp.where(
        live_rows, scaled_grad[slot_token], jnp.zeros((), scaled_grad.dtype)
    ).reshape(nblocks, BLOCK, width)
    slot_prob = prob[slot_token] * slot_live

    def project(rows_x, expert):
        gate_act = jnp.dot(rows_x, fetch(w_gate, expert), preferred_element_type=jnp.float32)
        up_act = jnp.dot(rows_x, fetch(w_up, expert), preferred_element_type=jnp.float32)
        return (gate_act, up_act)

    def forward_block(carry, inputs):
        rows_x, expert = inputs
        gate_act, up_act = project(rows_x, expert)
        hidden = (gate_act * jax.nn.sigmoid(gate_act) * up_act).astype(jnp.bfloat16)
        partial_out = jnp.dot(hidden, fetch(w_down, expert), preferred_element_type=jnp.float32)
        return (carry, (partial_out, hidden, gate_act, up_act))

    unused, forward = lax.scan(forward_block, jnp.zeros((), jnp.float32), (slot_x, block_expert))
    slot_out = forward[0].reshape(-1, width) * slot_prob[:, None]
    output = lax.psum_scatter(
        slot_out[token_slot], "shard", scatter_dimension=0, tiled=True
    ).astype(jnp.bfloat16)
    hiddens = forward[1]
    kept = (forward[2], forward[3])

    def input_terms(rows_dout, expert, stored):
        gate_act, up_act = stored
        gate_w = fetch(w_gate, expert)
        up_w = fetch(w_up, expert)
        back_hidden = jnp.dot(
            rows_dout, fetch(w_down, expert).T, preferred_element_type=jnp.float32
        )
        sigma = jax.nn.sigmoid(gate_act)
        gate_grad = (back_hidden * up_act * sigma * (1.0 + gate_act * (1.0 - sigma))).astype(
            jnp.bfloat16
        )
        up_grad = (back_hidden * (gate_act * sigma)).astype(jnp.bfloat16)
        in_grad = jnp.dot(gate_grad, gate_w.T, preferred_element_type=jnp.float32) + jnp.dot(
            up_grad, up_w.T, preferred_element_type=jnp.float32
        )
        return (gate_grad, up_grad, in_grad)

    zero_gate = jnp.zeros(w_gate.shape, jnp.float32)
    zero_up = jnp.zeros(w_up.shape, jnp.float32)
    zero_down = jnp.zeros(w_down.shape, jnp.float32)

    def proj_block(carry, inputs):
        grad_gate, grad_up = carry
        rows_x, rows_dout, expert, stored = inputs
        gate_grad, up_grad, in_grad = input_terms(rows_dout, expert, stored)
        grad_gate = add_at(
            grad_gate, expert, jnp.dot(rows_x.T, gate_grad, preferred_element_type=jnp.float32)
        )
        grad_up = add_at(
            grad_up, expert, jnp.dot(rows_x.T, up_grad, preferred_element_type=jnp.float32)
        )
        return ((grad_gate, grad_up), in_grad)

    def full_block(carry, inputs):
        grad_gate, grad_up, grad_down = carry
        rows_x, rows_dout, hidden, expert, stored = inputs
        grad_down = add_at(
            grad_down, expert, jnp.dot(hidden.T, rows_dout, preferred_element_type=jnp.float32)
        )
        pair, in_grad = proj_block((grad_gate, grad_up), (rows_x, rows_dout, expert, stored))
        return ((pair[0], pair[1], grad_down), in_grad)

    partials, in_grads = lax.scan(
        full_block,
        (zero_gate, zero_up, zero_down),
        (slot_x, slot_dout, hiddens, block_expert, kept),
    )
    grad_gate, grad_up, grad_down = (
        lax.psum_scatter(partials[0], "dp", scatter_dimension=1, tiled=True),
        lax.psum_scatter(partials[1], "dp", scatter_dimension=1, tiled=True),
        lax.psum_scatter(partials[2], "dp", scatter_dimension=2, tiled=True),
    )
    slot_in = in_grads.reshape(-1, width)
    input_grad = lax.psum_scatter(
        slot_in[token_slot], "shard", scatter_dimension=0, tiled=True
    ).astype(jnp.bfloat16)
    return (output, input_grad, grad_gate, grad_up, grad_down)


def solution(mesh):
    placed = (
        P(("dp", "shard"), None),
        P(("dp", "shard"), None),
        P("dp"),
        P("dp"),
        P(None, None, "shard"),
        P(None, None, "shard"),
        P(None, "shard", None),
    )
    return jax.shard_map(
        per_device,
        mesh=mesh,
        in_specs=placed,
        out_specs=(
            P(("dp", "shard"), None),
            P(("dp", "shard"), None),
            P(None, "dp", "shard"),
            P(None, "dp", "shard"),
            P(None, "shard", "dp"),
        ),
        check_vma=False,
    )
```

profile of v0, /device:TPU:0, one launch (start us, length us, event | category | flops | bytes accessed | tf_op | source)
XLA Modules:
  0.0 892.2 jit_solution(2198746751006499723)
XLA Ops:
  17.4 10.3 %all_gather.6 = bf16[256,1024]{1,0:T(8,128)(2,1)S(1)} all-gather(bf16[128,1024]{1,0:T(8,128)(2,1)} %param.11), channel_id=1, replica_groups=mesh['dp'=16,'shard'=2] {'shard'}, dimensions={0}, use_global_device_ids=true | all-gather | bytes 786432 | tf_op jit(solution)/shard_map/all_gather | solution.py:48
  29.8 8.2 all_gather.7
  41.5 37.5 %while.32 = (s32[]{:T(128)}, f32[3,128,1024]{2,1,0:T(8,128)S(1)}, bf16[3,128,2048]{2,1,0:T(8,128)(2,1)}, f32[3,128,2048]{2,1,0:T(8,128)}, f32[3,128,2048]{2,1,0:...) while((s32[]{:T(128)}, f32[3,128,1024]{2,1,0:T(8,128)S(1)}, ...), condition=%wide.region_10.11_spmd, body=%wide.region_9.10_spmd.sunk | while | flops 1612185600 | bytes 46664940 | solution.py:75
  82.6 8.0 broadcast.194.clone
  90.6 7.8 broadcast.194
  106.3 207.9 %while.33 = (s32[]{:T(128)}, f32[2,1024,2048]{2,1,0:T(8,128)}, f32[2,1024,2048]{2,1,0:T(8,128)}, f32[2,2048,1024]{1,2,0:T(8,128)}, f32[3,128,1024]{2,1,0:T(8,128...) while((s32[]{:T(128)}, f32[2,1024,2048]{2,1,0:T(8,128)}, ...), condition=%wide.region_13.14_spmd, body=%wide.region_12.13_spmd.sunk | while | flops 3231055872 | bytes 322964320 | solution.py:125
  125.5 9.2 %copy.22 = f32[1,2048,1024]{2,1,0:T(8,128)} copy(f32[1,2048,1024]{1,2,0:T(8,128)} %constant_dynamic-slice_fusion.2) | data formatting | bytes 16777216 | tf_op jit(solution)/shard_map/while/body/eval_jaxpr/jit(dynamic_index_in_dim)/dynamic_slice | solution.py:37
  134.8 8.1 bitcast_add_fusion.4
  142.9 9.1 %copy.23 = f32[1,2048,1024]{1,2,0:T(8,128)} copy(f32[1,2048,1024]{2,1,0:T(8,128)} %bitcast_add_fusion.4) | data formatting | bytes 16777216 | tf_op jit(solution)/shard_map/while/body/eval_jaxpr/jit(dynamic_update_index_in_dim)/dynamic_update_slice | solution.py:38
  152.0 7.8 constant_dynamic-update-slice_fusion.2
  159.8 8.0 fusion.111
  194.9 9.2 %copy.22 = f32[1,2048,1024]{2,1,0:T(8,128)} copy(f32[1,2048,1024]{1,2,0:T(8,128)} %constant_dynamic-slice_fusion.2) | data formatting | bytes 16777216 | tf_op jit(solution)/shard_map/while/body/eval_jaxpr/jit(dynamic_index_in_dim)/dynamic_slice | solution.py:37
  204.1 8.1 bitcast_add_fusion.4
  212.2 9.1 %copy.23 = f32[1,2048,1024]{1,2,0:T(8,128)} copy(f32[1,2048,1024]{2,1,0:T(8,128)} %bitcast_add_fusion.4) | data formatting | bytes 16777216 | tf_op jit(solution)/shard_map/while/body/eval_jaxpr/jit(dynamic_update_index_in_dim)/dynamic_update_slice | solution.py:38
  229.2 8.0 fusion.111
  264.2 9.2 %copy.22 = f32[1,2048,1024]{2,1,0:T(8,128)} copy(f32[1,2048,1024]{1,2,0:T(8,128)} %constant_dynamic-slice_fusion.2) | data formatting | bytes 16777216 | tf_op jit(solution)/shard_map/while/body/eval_jaxpr/jit(dynamic_index_in_dim)/dynamic_slice | solution.py:37
  273.4 8.1 bitcast_add_fusion.4
  281.5 9.1 %copy.23 = f32[1,2048,1024]{1,2,0:T(8,128)} copy(f32[1,2048,1024]{2,1,0:T(8,128)} %bitcast_add_fusion.4) | data formatting | bytes 16777216 | tf_op jit(solution)/shard_map/while/body/eval_jaxpr/jit(dynamic_update_index_in_dim)/dynamic_update_slice | solution.py:38
  290.6 7.8 constant_dynamic-update-slice_fusion.2
  298.5 8.0 fusion.111
  320.2 17.9 %reduce-scatter.8.cloned.1.call-done = f32[128,1024]{1,0:T(8,128)} async-done(((f32[256,1024]{1,0:T(8,128)}), f32[128,1024]{1,0:T(8,128)}) %reduce-scatter.8.cloned.1.call-update) | async-done | bytes 524304 | tf_op jit(solution)/shard_map/reduce_scatter | solution.py:136
  339.8 181.5 %reduce-scatter.10.cloned.1.call-done = f32[2,64,2048]{2,1,0:T(8,128)} async-done(((f32[2,1024,2048]{2,1,0:T(8,128)}), f32[2,64,2048]{2,1,0:T(8,128)}) %reduce-scatter.10.cloned.1.call-update) | async-done | bytes 1048592 | tf_op jit(solution)/shard_map/reduce_scatter | solution.py:131
  521.3 182.2 %reduce-scatter.12.cloned.1.call-done = f32[2,64,2048]{2,1,0:T(8,128)} async-done(((f32[2,1024,2048]{2,1,0:T(8,128)}), f32[2,64,2048]{2,1,0:T(8,128)}) %reduce-scatter.12.cloned.1.call-update) | async-done | bytes 1048592 | tf_op jit(solution)/shard_map/reduce_scatter | solution.py:132
  703.5 182.1 %reduce-scatter.14.cloned.1.call-done = f32[2,2048,64]{1,2,0:T(8,128)} async-done(((f32[2,2048,1024]{1,2,0:T(8,128)}), f32[2,2048,64]{1,2,0:T(8,128)}) %reduce-scatter.14.cloned.1.call-update) | async-done | bytes 1048592 | tf_op jit(solution)/shard_map/reduce_scatter | solution.py:133
  (148 shorter events, 149.0 us)
Async XLA Ops:
  7.2 311.2 %reduce-scatter.6.cloned.1.call-start = ((), (), s32[]{:S(2)}) async-start(), calls=%async_computation.5 | async-start | bytes 1572864 | tf_op jit(solution)/shard_map/reduce_scatter | solution.py:77
  10.9 69.2 %copy-start.6 = (s32[1024]{0:T(1024)}, s32[1024]{0:T(1024)S(1)}, u32[]{:S(2)}) copy-start(s32[1024]{0:T(1024)S(1)} %pad_clamp_fusion) | copy-start | bytes 12292
  17.4 12.4 %copy-start.5 = (bf16[128,1024]{1,0:T(8,128)(2,1)S(1)}, bf16[128,1024]{1,0:T(8,128)(2,1)}, u32[]{:S(2)}) copy-start(bf16[128,1024]{1,0:T(8,128)(2,1)} %param.12) | copy-start | bytes 786436
  17.4 20.6 %copy-start = (f32[256]{0:T(256)S(1)}, f32[256]{0:T(256)}, u32[]{:S(2)}) copy-start(f32[256]{0:T(256)} %param.14) | copy-start | bytes 3076
  44.0 8.1 slice-start.4
  56.5 8.2 slice-start.4
  69.0 8.2 slice-start.4
  82.2 255.8 %reduce-scatter.8.cloned.1.call-start = ((), (), s32[]{:S(2)}) async-start(), calls=%async_computation.6 | async-start | bytes 1572864 | tf_op jit(solution)/shard_map/reduce_scatter | solution.py:136
  108.8 12.9 %copy-start.1 = (f32[2,2048,1024]{1,2,0:T(8,128)S(1)}, f32[2,2048,1024]{1,2,0:T(8,128)}, u32[]{:S(2)}) copy-start(f32[2,2048,1024]{1,2,0:T(8,128)} %get-tuple-element.421) | copy-start | bytes 50331652 | tf_op jit(solution)/shard_map/while
  152.0 15.9 %slice-start = ((s8[16777216]{0:T(1024)(128)(4,1)}), s8[4194304]{0:T(1024)(128)(4,1)S(1)}, s32[]{:S(2)}) async-start(s8[16777216]{0:T(1024)(128)(4,1)} %bitcast.210), calls=%async_computation.10 | async-start | bytes 8388608 | tf_op jit(solution)/shard_map/while
  152.0 15.9 %slice-start.1 = ((s8[16777216]{0:T(1024)(128)(4,1)}), s8[4194304]{0:T(1024)(128)(4,1)S(1)}, s32[]{:S(2)}) async-start(s8[16777216]{0:T(1024)(128)(4,1)} %bitcast.210), calls=%async_computation.11 | async-start | bytes 8388608 | tf_op jit(solution)/shard_map/while
  159.8 8.0 slice-start.2
  159.8 8.0 slice-start.3
  178.2 12.9 %copy-start.1 = (f32[2,2048,1024]{1,2,0:T(8,128)S(1)}, f32[2,2048,1024]{1,2,0:T(8,128)}, u32[]{:S(2)}) copy-start(f32[2,2048,1024]{1,2,0:T(8,128)} %get-tuple-element.421) | copy-start | bytes 50331652 | tf_op jit(solution)/shard_map/while
  221.3 15.9 %slice-start = ((s8[16777216]{0:T(1024)(128)(4,1)}), s8[4194304]{0:T(1024)(128)(4,1)S(1)}, s32[]{:S(2)}) async-start(s8[16777216]{0:T(1024)(128)(4,1)} %bitcast.210), calls=%async_computation.10 | async-start | bytes 8388608 | tf_op jit(solution)/shard_map/while
  221.3 15.9 %slice-start.1 = ((s8[16777216]{0:T(1024)(128)(4,1)}), s8[4194304]{0:T(1024)(128)(4,1)S(1)}, s32[]{:S(2)}) async-start(s8[16777216]{0:T(1024)(128)(4,1)} %bitcast.210), calls=%async_computation.11 | async-start | bytes 8388608 | tf_op jit(solution)/shard_map/while
  229.2 8.0 slice-start.3
  247.5 12.9 %copy-start.1 = (f32[2,2048,1024]{1,2,0:T(8,128)S(1)}, f32[2,2048,1024]{1,2,0:T(8,128)}, u32[]{:S(2)}) copy-start(f32[2,2048,1024]{1,2,0:T(8,128)} %get-tuple-element.421) | copy-start | bytes 50331652 | tf_op jit(solution)/shard_map/while
  290.6 15.9 %slice-start = ((s8[16777216]{0:T(1024)(128)(4,1)}), s8[4194304]{0:T(1024)(128)(4,1)S(1)}, s32[]{:S(2)}) async-start(s8[16777216]{0:T(1024)(128)(4,1)} %bitcast.210), calls=%async_computation.10 | async-start | bytes 8388608 | tf_op jit(solution)/shard_map/while
  290.6 15.9 %slice-start.1 = ((s8[16777216]{0:T(1024)(128)(4,1)}), s8[4194304]{0:T(1024)(128)(4,1)S(1)}, s32[]{:S(2)}) async-start(s8[16777216]{0:T(1024)(128)(4,1)} %bitcast.210), calls=%async_computation.11 | async-start | bytes 8388608 | tf_op jit(solution)/shard_map/while
  298.5 8.0 slice-start.3
  316.4 204.9 %reduce-scatter.10.cloned.1.call-start = ((), (), s32[]{:S(2)}) async-start(), calls=%async_computation.7 | async-start | bytes 17825792 | tf_op jit(solution)/shard_map/reduce_scatter | solution.py:131
  317.2 386.3 %reduce-scatter.12.cloned.1.call-start = ((), (), s32[]{:S(2)}) async-start(), calls=%async_computation.8 | async-start | bytes 17825792 | tf_op jit(solution)/shard_map/reduce_scatter | solution.py:132
  317.8 567.9 %reduce-scatter.14.cloned.1.call-start = ((), (), s32[]{:S(2)}) async-start(), calls=%async_computation.9 | async-start | bytes 17825792 | tf_op jit(solution)/shard_map/reduce_scatter | solution.py:133
  (10 other events, 54.2 us)
Sparse Core Ops, SparseCore 0:
  82.3 21.4 reduce-scatter.5
  316.6 21.4 reduce-scatter.7
  342.7 178.5 reduce-scatter.9
  525.9 177.5 reduce-scatter.11
  708.1 177.5 reduce-scatter.13
where the time goes:
time: 893 us; the launch traced here: 892 us
  waiting for transfers between devices  566 us (63%)
  local copies, waits for them, and re-layouts  154 us (17%)
  matrix products  120 us (13%)
  blocking collectives  18.5 us (2%)
  between operations  14 us (2%)
  loops' own time  12 us (1%)
    reduce_scatter x1, waiting for transfers between devices, per_device(): lax.psum_scatter(partials[1], 'dp', scatter_dimension=1, tiled=True)  182 us
    reduce_scatter x1, waiting for transfers between devices, per_device(): lax.psum_scatter(partials[2], 'dp', scatter_dimension=2, tiled=True)  182 us
    reduce_scatter x1, waiting for transfers between devices, per_device(): lax.psum_scatter(partials[0], 'dp', scatter_dimension=1, tiled=True)  182 us
    dynamic_update_slice x6, local copies, waits for them, and re-layouts, add_at(): return lax.dynamic_update_index_in_dim(total, old + term[None], expert, 0)  50.8 us
    dynamic_slice x6, local copies, waits for them, and re-layouts, add_at(): old = lax.dynamic_index_in_dim(total, expert, 0, keepdims=True)  39.1 us
    dot_general x3, matrix products, full_block(): jnp.dot(hidden.T, rows_dout, preferred_element_type=jnp.float32)  24.3 us
    dot_general x3, matrix products, proj_block(): jnp.dot(rows_x.T, gate_grad, preferred_element_type=jnp.float32)  24.1 us
    reduce_scatter x1, waiting for transfers between devices, per_device(): lax.psum_scatter(slot_in[token_slot], 'shard', scatter_dimension=0, tiled...  17.9 us
  transfers between devices with their start and end apart: 5, of which 4 were waited for; matrix products, arithmetic and copies ran while one was open for 24% of the time, Pallas kernels for 0%

commit v1 on v0

v1 whole, which is shorter than its diff:
```python
import functools

import jax
import jax.numpy as jnp
from jax import lax
from jax.experimental import pallas as pl
from jax.experimental.pallas import tpu as pltpu
from jax.sharding import PartitionSpec as P

EXP = 2
NZ = 4
CHUNK = 256
MESH = pl.DeviceIdType.MESH
LAG = 1


def wgrad_kernel(
    nx, fac, xst, out, gbuf, xbuf, psend, prec, pacc, g_send, g_recv, x_send, x_recv, z_send, z_recv
):
    ng = 2 * nx
    nq = fac.shape[0]
    me = lax.axis_index("dp")
    z = me // ng
    slot = me % ng
    xi = slot // 2
    core = slot % 2
    other = z * ng + xi * 2 + (1 - core)

    barrier = pltpu.get_barrier_semaphore()
    for d in range(1, ng):
        peer = z * ng + (slot + d) % ng
        pl.semaphore_signal(barrier, inc=1, device_id={"dp": peer}, device_id_type=MESH)
    for d in range(1, NZ):
        peer = ((z + d) % NZ) * ng + slot
        pl.semaphore_signal(barrier, inc=1, device_id={"dp": peer}, device_id_type=MESH)
    pl.semaphore_wait(barrier, ng - 1 + NZ - 1)

    def remote(src, dst, send, recv, peer):
        return pltpu.make_async_remote_copy(
            src_ref=src,
            dst_ref=dst,
            send_sem=send,
            recv_sem=recv,
            device_id={"dp": peer},
            device_id_type=MESH,
        )

    def x_copy(d):
        to = (slot + d) % ng
        return remote(xst.at[to], xbuf.at[slot], x_send.at[d], x_recv.at[slot], z * ng + to)

    def x_arrival(d):
        s = (slot + d) % ng
        return remote(xst.at[s], xbuf.at[s], x_send.at[d], x_recv.at[s], z * ng + s)

    def g_copy(q, k):
        peer = other if k == 0 else z * ng + ((xi + k) % nx) * 2 + core
        return remote(fac.at[q], gbuf.at[q, slot], g_send.at[q, k], g_recv.at[q, slot], peer)

    def g_forward(q, k):
        s = ((xi + k) % nx) * 2 + core
        return remote(
            gbuf.at[q, s], gbuf.at[q, s], g_send.at[q, nx - 1 + k], g_recv.at[q, s], other
        )

    def g_arrival(q, s):
        return remote(gbuf.at[q, s], gbuf.at[q, s], g_send.at[q, 0], g_recv.at[q, s], other)

    def z_copy(q, d):
        to = (z + d) % NZ
        return remote(
            psend.at[q, to], prec.at[q, z], z_send.at[q, d], z_recv.at[q, z], to * ng + slot
        )

    def z_arrival(q, d):
        s = (z + d) % NZ
        return remote(
            psend.at[q, s], prec.at[q, s], z_send.at[q, d], z_recv.at[q, s], s * ng + slot
        )

    for d in range(1, ng):
        x_copy(d).start()

    def send_own(q, carry):
        for k in range(nx):
            g_copy(q, k).start()
        return carry

    lax.fori_loop(0, nq, send_own, 0)
    xbuf[slot] = xst[slot]
    for d in range(1, ng):
        x_arrival(d).wait_recv()

    def forward(q):
        for k in range(1, nx):
            g_arrival(q, ((xi + k) % nx) * 2 + core).wait_recv()
            g_forward(q, k).start()

    def compute(q):
        gbuf[q, slot] = fac[q]
        for k in range(nx):
            g_arrival(q, ((xi + k) % nx) * 2 + (1 - core)).wait_recv()
        side = (q % 3) // 2
        part = jnp.dot(xbuf[0, side], gbuf[q, 0], preferred_element_type=jnp.float32)
        for s in range(1, ng):
            part = part + jnp.dot(xbuf[s, side], gbuf[q, s], preferred_element_type=jnp.float32)
        part = part.reshape(pacc.shape)
        pacc[...] = part
        psend[q] = part.astype(jnp.bfloat16)
        for d in range(1, NZ):
            z_copy(q, d).start()
        out[q] = pacc[z]

    for q in range(LAG):
        forward(q)

    def step(q, carry):
        forward(q + LAG)
        compute(q)
        return carry

    lax.fori_loop(0, nq - LAG, step, 0)

    def last(q, carry):
        compute(q)
        return carry

    lax.fori_loop(nq - LAG, nq, last, 0)

    def finish(q, carry):
        total = out[q]
        for d in range(1, NZ):
            z_arrival(q, d).wait_recv()
            total = total + prec[q, (z + d) % NZ].astype(jnp.float32)
        out[q] = total
        for k in range(nx):
            g_copy(q, k).wait_send()
        for k in range(1, nx):
            g_forward(q, k).wait_send()
        for d in range(1, NZ):
            z_copy(q, d).wait_send()
        return carry

    lax.fori_loop(0, nq, finish, 0)
    for d in range(1, ng):
        x_copy(d).wait_send()


def weight_grads(nx, fac, xst):
    nq, rows, chunk = fac.shape
    ng = 2 * nx
    own = xst.shape[2] // NZ
    vmem = pl.BlockSpec(memory_space=pltpu.VMEM)
    flops = 2 * nq * ng * rows * chunk * xst.shape[2]
    return pl.pallas_call(
        functools.partial(wgrad_kernel, nx),
        out_shape=jax.ShapeDtypeStruct((nq, own, chunk), jnp.float32),
        in_specs=[vmem, vmem],
        out_specs=vmem,
        scratch_shapes=[
            pltpu.VMEM((nq, ng, rows, chunk), jnp.bfloat16),
            pltpu.VMEM(xst.shape, jnp.bfloat16),
            pltpu.VMEM((nq, NZ, own, chunk), jnp.bfloat16),
            pltpu.VMEM((nq, NZ, own, chunk), jnp.bfloat16),
            pltpu.VMEM((NZ, own, chunk), jnp.float32),
            pltpu.SemaphoreType.DMA((nq, 2 * nx)),
            pltpu.SemaphoreType.DMA((nq, ng)),
            pltpu.SemaphoreType.DMA((ng,)),
            pltpu.SemaphoreType.DMA((ng,)),
            pltpu.SemaphoreType.DMA((nq, NZ)),
            pltpu.SemaphoreType.DMA((nq, NZ)),
        ],
        compiler_params=pltpu.CompilerParams(
            collective_id=0, has_side_effects=True, vmem_limit_bytes=56 * 1024 * 1024
        ),
        cost_estimate=pl.CostEstimate(
            flops=flops, bytes_accessed=400_000_000, transcendentals=0
        ),
    )(fac, xst)


def per_device(dp, tokens, cotangent, assign, prob, w_gate, w_up, w_down):
    width = tokens.shape[1]
    local_ff = w_gate.shape[2]
    nx = dp // (2 * NZ)
    ng = 2 * nx
    own = width // dp
    nc = local_ff // CHUNK
    f32, bf16 = jnp.float32, jnp.bfloat16

    both = lax.all_gather(jnp.stack([tokens, cotangent]), "shard", axis=1, tiled=True)
    x, dout = both[0], both[1]
    rows = x.shape[0]
    scaled = (prob[:, None] * dout.astype(f32)).astype(bf16)
    live = [(assign == e)[:, None] for e in range(EXP)]
    zero = jnp.zeros((), bf16)
    xs = [jnp.where(m, x, zero) for m in live]
    gs = [jnp.where(m, scaled, zero) for m in live]

    def pick(terms):
        total = terms[-1]
        for e in range(EXP - 1):
            total = jnp.where(live[e], terms[e], total)
        return total

    xcat = jnp.concatenate(xs, axis=1)
    gate = jnp.dot(xcat, w_gate.reshape(EXP * width, local_ff), preferred_element_type=f32)
    up = jnp.dot(xcat, w_up.reshape(EXP * width, local_ff), preferred_element_type=f32)
    back = sum(
        lax.dot_general(gs[e], w_down[e], (((1,), (1,)), ((), ())), preferred_element_type=f32)
        for e in range(EXP)
    )
    sigma = jax.nn.sigmoid(gate)
    act = gate * sigma
    hidden = (act * up).astype(bf16)
    gate_grad = (back * up * sigma * (1.0 + gate * (1.0 - sigma))).astype(bf16)
    up_grad = (back * act).astype(bf16)

    fac = jnp.stack([gate_grad, up_grad, hidden])
    fac = fac.reshape(3, rows, nc, CHUNK).transpose(2, 0, 1, 3).reshape(3 * nc, rows, CHUNK)
    xst = jnp.stack([jnp.stack(xs), jnp.stack(gs)])
    xst = xst.reshape(2, EXP, rows, NZ, ng, own).transpose(4, 0, 3, 1, 5, 2)
    xst = xst.reshape(ng, 2, NZ * EXP * own, rows)
    grads = weight_grads(nx, fac, xst).reshape(nc, 3, EXP, own, CHUNK)
    grad_gate = grads[:, 0].transpose(1, 2, 0, 3).reshape(EXP, own, local_ff)
    grad_up = grads[:, 1].transpose(1, 2, 0, 3).reshape(EXP, own, local_ff)
    grad_down = grads[:, 2].transpose(1, 0, 3, 2).reshape(EXP, local_ff, own)

    part_out = pick([jnp.dot(hidden, w_down[e], preferred_element_type=f32) for e in range(EXP)])
    contract = (((1,), (1,)), ((), ()))
    part_in = pick(
        [
            lax.dot_general(gate_grad, w_gate[e], contract, preferred_element_type=f32)
            + lax.dot_general(up_grad, w_up[e], contract, preferred_element_type=f32)
            for e in range(EXP)
        ]
    )
    sums = lax.psum_scatter(
        jnp.stack([part_out * prob[:, None], part_in]), "shard", scatter_dimension=1, tiled=True
    ).astype(bf16)
    return (sums[0], sums[1], grad_gate, grad_up, grad_down)


def solution(mesh):
    placed = (
        P(("dp", "shard"), None),
        P(("dp", "shard"), None),
        P("dp"),
        P("dp"),
        P(None, None, "shard"),
        P(None, None, "shard"),
        P(None, "shard", None),
    )
    return jax.shard_map(
        functools.partial(per_device, mesh.shape["dp"]),
        mesh=mesh,
        in_specs=placed,
        out_specs=(
            P(("dp", "shard"), None),
            P(("dp", "shard"), None),
            P(None, "dp", "shard"),
            P(None, "dp", "shard"),
            P(None, "shard", "dp"),
        ),
        check_vma=False,
    )
```

time: 893 us -> 269 us (0.30)
  waiting for transfers between devices: 566 us -> 24.3 us
  Pallas kernels: 0 us -> 177 us
  local copies, waits for them, and re-layouts: 154 us -> 17.7 us
  matrix products: 120 us -> 21.8 us
  blocking collectives: 18.5 us -> 0 us
  loops' own time: 12 us -> 0 us
    reduce_scatter x5 -> x1, waiting for transfers between devices: 564 us -> 0.01 us  [per_device(): lax.psum_scatter(jnp.stack([part_out * prob[:, None], part_in]), 'shard',...]
    pallas_call x0 -> x1, Pallas kernels: none -> 177 us  [weight_grads(): pl.pallas_call(functools.partial(wgrad_kernel, nx), out_shape=jax.ShapeDt...]
    dot_general x27 -> x10, matrix products: 120 us -> 21.8 us  [the longest x2 5.35 us: per_device(): lax.dot_general(gs[e], w_down[e], (((1,), (1,)), ((), ())), preferred_ele...]
    dynamic_update_slice x9 -> x0, local copies, waits for them, and re-layouts: 54.1 us -> none  [the longest x6 50.8 us: add_at(): return lax.dynamic_update_index_in_dim(total, old + term[None], expert, 0)]
    dynamic_slice x12 -> x0, local copies, waits for them, and re-layouts: 42.6 us -> none  [the longest x6 39.1 us: add_at(): old = lax.dynamic_index_in_dim(total, expert, 0, keepdims=True)]
    all_gather x0 -> x1, waiting for transfers between devices: none -> 24.3 us  [per_device(): lax.all_gather(jnp.stack([tokens, cotangent]), 'shard', axis=1, tiled=True)]
    all_gather x2 -> x0, blocking collectives: 18.5 us -> none  [the longest x1 10.3 us: per_device(): lax.all_gather(tokens, 'shard', axis=0, tiled=True)]
    while x48 -> x0, local copies, waits for them, and re-layouts: 17.2 us -> none
  transfers between devices with their start and end apart: 5 -> 2, of which waited for: 4 -> 1; matrix products, arithmetic and copies ran while one was open for 24% -> 7% of each run, Pallas kernels for 0% -> 66%
where the time goes in v1:
time: 269 us; the launch traced here: 268 us
  Pallas kernels  177 us (66%)
  waiting for transfers between devices  24.3 us (9%)
  matrix products  21.8 us (8%)
  local copies, waits for them, and re-layouts  17.7 us (7%)
  between operations  14.3 us (5%)
  other arithmetic  13.2 us (5%)
    pallas_call x1, Pallas kernels, weight_grads(): pl.pallas_call(functools.partial(wgrad_kernel, nx), out_shape=jax.ShapeDt...  177 us
    all_gather x1, waiting for transfers between devices, per_device(): lax.all_gather(jnp.stack([tokens, cotangent]), 'shard', axis=1, tiled=True)  24.3 us
    unnamed x26, local copies, waits for them, and re-layouts  5.89 us
  transfers between devices with their start and end apart: 2, of which 1 were waited for; matrix products, arithmetic and copies ran while one was open for 7% of the time, Pallas kernels for 66%

profile of v1, /device:TPU:0, one launch (start us, length us, event | category | flops | bytes accessed | tf_op | source)
XLA Modules:
  0.0 268.3 jit_solution(7513779704414899121)
XLA Ops:
  7.2 1.9 pad_maximum_fusion.7
  9.8 24.3 %all-gather.2.cloned.1.call-done = bf16[2,256,1024]{2,1,0:T(8,128)(2,1)} async-done(((bf16[2,128,1024]{2,1,0:T(8,128)(2,1)}), bf16[2,256,1024]{2,1,0:T(8,128)(2,1)}) %all-gather.2.cloned.1.call-update) | async-done | bytes 1048592 | tf_op jit(solution)/shard_map/all_gather | solution.py:191
  34.2 2.5 broadcast_select_fusion.3
  36.7 4.0 %fusion.8 = f32[256,2048]{1,0:T(8,128)S(1)} fusion(bf16[2,2048,1024]{2,1,0:T(8,128)(2,1)} %param.13, bf16[1,256,1024]{2,1,0:T(8,128)(2,1)S(1)} %get-tuple-element.12), kind=kOutput, calls=%fused_computation.8 | convolution fusion | flops 1073741824 | bytes 6815744 | tf_op jit(solution)/shard_map/dot_general | solution.py:210
  40.8 1.3 fusion.24
  42.3 2.2 copy-done.8
  44.5 3.7 %fusion.50 = f32[256,2048]{1,0:T(8,128)} fusion(bf16[2048,2048]{1,0:T(8,128)(2,1)S(1)} %bitcast.122, bf16[256,1024]{1,0:T(8,128)(2,1)S(1)} %get-tuple-element.16, bf16[256,1024]{1,0:T(8,128)(2,1)S(1)} %get-tuple-element.15), kind=kOutput, calls=%fused_computation.48 | convolution fusion | flops 2149580800 | bytes 11534336 | tf_op jit(solution)/shard_map/dot_general | solution.py:207
  48.2 4.8 %multiply_convert_fusion.2 = (bf16[256,2048]{1,0:T(8,128)(2,1)S(1)}, bf16[256,2048]{1,0:T(8,128)(2,1)S(1)}, bf16[256,2048]{1,0:T(8,128)(2,1)S(1)}) fusion(f32[256,2048]{1,0:T(8,128)} %fusion.50, f32[256,2048]{1,0:T(8,128)S(1)} %fusion.24, bf16[2048,2048]{1,0:T(8,128)(2,1)S(1)} %bitcast.121, bf16[256,1024]{1,0:T(8,128)(2,1)S(1)} %get-tuple-element.16, ...), kind=kOutput, calls=%fused_computation.30 | convolution fusion | flops 2157445120 | bytes 16777216 | tf_op jit(solution)/shard_map/dot_general | solution.py:208
  53.0 1.3 fusion.4
  54.3 1.3 fusion
  55.6 1.3 fusion.10
  56.9 1.3 fusion.46
  58.2 1.5 fusion.28
  59.7 1.3 fusion.37
  61.0 1.5 pad_maximum_fusion.1
  65.6 1.5 pad_maximum_fusion.3
  67.1 2.3 copy.24
  69.4 2.3 copy.23
  71.7 1.7 maximum_bitcast_fusion
  73.4 1.5 copy.25
  75.0 2.0 pad_maximum_fusion
  77.0 176.8 %shard_map.110 = f32[24,128,256]{2,1,0:T(8,128)} custom-call(bf16[24,256,256]{2,1,0:T(8,128)(2,1)} %bitcast.109, bf16[4,2,512,256]{3,2,1,0:T(8,128)(2,1)} %bitcast.110), custom_call_target="tpu_custom_call" | custom-call | flops 6442450944 | bytes 400000000 | tf_op jit(solution)/shard_map/pallas_call | solution.py:155
  253.8 2.2 slice_bitcast_fusion
  259.3 1.3 convert_element_type.31
  (39 shorter events, 8.1 us)
Async XLA Ops:
  7.2 27.0 %all-gather.2.cloned.1.call-start = ((), (), s32[]{:S(2)}) async-start(), calls=%async_computation.1 | async-start | bytes 1572864 | tf_op jit(solution)/shard_map/all_gather | solution.py:191
  9.1 250.2 %reduce-scatter.2.cloned.1.call-start = ((), (), s32[]{:S(2)}) async-start(), calls=%async_computation.2 | async-start | bytes 3145728 | tf_op jit(solution)/shard_map/reduce_scatter | solution.py:238
  34.2 6.6 %copy-start.2 = (bf16[2,2048,1024]{2,1,0:T(8,128)(2,1)S(1)}, bf16[2,2048,1024]{2,1,0:T(8,128)(2,1)}, u32[]{:S(2)}) copy-start(bf16[2,2048,1024]{2,1,0:T(8,128)(2,1)} %param.13) | copy-start | bytes 25165828
  40.7 1.3 copy-start.1
  40.8 3.7 %copy-start.8 = (bf16[2,1024,2048]{2,1,0:T(8,128)(2,1)S(1)}, bf16[2,1024,2048]{2,1,0:T(8,128)(2,1)}, u32[]{:S(2)}) copy-start(bf16[2,1024,2048]{2,1,0:T(8,128)(2,1)} %param.11) | copy-start | bytes 25165828
  42.1 6.1 %slice-start = ((s8[8388608]{0:T(1024)(128)(4,1)}), s8[4194304]{0:T(1024)(128)(4,1)S(1)}, s32[]{:S(2)}) async-start(s8[8388608]{0:T(1024)(128)(4,1)} %bitcast.119), calls=%async_computation.3 | async-start | bytes 8388608
  44.5 3.7 %slice-start.1 = ((s8[8388608]{0:T(1024)(128)(4,1)}), s8[4194304]{0:T(1024)(128)(4,1)S(1)}, s32[]{:S(2)}) async-start(s8[8388608]{0:T(1024)(128)(4,1)} %bitcast.119), calls=%async_computation.4 | async-start | bytes 8388608
  53.0 6.7 %copy-start.5 = (bf16[256,2048]{1,0:T(8,128)(2,1)}, bf16[256,2048]{1,0:T(8,128)(2,1)S(1)}, u32[]{:S(2)}) copy-start(bf16[256,2048]{1,0:T(8,128)(2,1)S(1)} %get-tuple-element.6) | copy-start | bytes 3145732
  55.6 1.3 copy-start.7
  62.9 1.2 copy-start.6
  63.4 2.2 copy-start.3
  63.4 2.2 copy-start.4
  73.4 1.6 copy-start
Sparse Core Ops, SparseCore 0:
  10.1 23.9 all-gather.1
  62.7 31.8 reduce-scatter.1

commit v2 on v1

--- a/solution.py
+++ b/solution.py
@@ -179,7 +179,7 @@
     )(fac, xst)
 
 
-def per_device(dp, tokens, cotangent, assign, prob, w_gate, w_up, w_down):
+def per_device(dp, shards, tokens, cotangent, assign, prob, w_gate, w_up, w_down):
     width = tokens.shape[1]
     local_ff = w_gate.shape[2]
     nx = dp // (2 * NZ)
@@ -188,7 +188,14 @@
     nc = local_ff // CHUNK
     f32, bf16 = jnp.float32, jnp.bfloat16
 
-    both = lax.all_gather(jnp.stack([tokens, cotangent]), "shard", axis=1, tiled=True)
+    mine = jnp.stack([tokens, cotangent])
+    block = mine.shape[1]
+    at = lax.axis_index("shard")
+    both = jnp.zeros((2, shards * block, width), bf16)
+    both = lax.dynamic_update_slice_in_dim(both, mine, at * block, 1)
+    for hop in range(1, shards):
+        got = lax.ppermute(mine, "shard", [(i, (i + hop) % shards) for i in range(shards)])
+        both = lax.dynamic_update_slice_in_dim(both, got, ((at - hop) % shards) * block, 1)
     x, dout = both[0], both[1]
     rows = x.shape[0]
     scaled = (prob[:, None] * dout.astype(f32)).astype(bf16)
@@ -252,7 +259,7 @@
         P(None, "shard", None),
     )
     return jax.shard_map(
-        functools.partial(per_device, mesh.shape["dp"]),
+        functools.partial(per_device, mesh.shape["dp"], mesh.shape["shard"]),
         mesh=mesh,
         in_specs=placed,
         out_specs=(

time: 269 us -> 257 us (0.955)
  waiting for transfers between devices: 24.3 us -> 11.3 us
  starting transfers between devices: 0.08 us -> 3.07 us
    all_gather x1 -> x0, waiting for transfers between devices: 24.3 us -> none  [per_device(): lax.all_gather(jnp.stack([tokens, cotangent]), 'shard', axis=1, tiled=True)]
    ppermute x0 -> x1, waiting for transfers between devices: none -> 11.2 us  [per_device(): lax.ppermute(mine, 'shard', [(i, (i + hop) % shards) for i in range(shard...]
    ppermute x0 -> x1, starting transfers between devices: none -> 3.03 us  [per_device(): lax.ppermute(mine, 'shard', [(i, (i + hop) % shards) for i in range(shard...]
    unnamed x26 -> x32, local copies, waits for them, and re-layouts: 5.89 us -> 5.28 us
  transfers between devices with their start and end apart: 2 -> 2, of which waited for: 1 -> 1; matrix products, arithmetic and copies ran while one was open for 7% -> 8% of each run, Pallas kernels for 66% -> 69%
where the time goes in v2:
time: 257 us; the launch traced here: 256 us
  Pallas kernels  177 us (69%)
  matrix products  21.6 us (8%)
  local copies, waits for them, and re-layouts  17.4 us (7%)
  between operations  14.4 us (6%)
  other arithmetic  11.3 us (4%)
  waiting for transfers between devices  11.3 us (4%)
  starting transfers between devices  3.07 us (1%)
    pallas_call x1, Pallas kernels, weight_grads(): pl.pallas_call(functools.partial(wgrad_kernel, nx), out_shape=jax.ShapeDt...  177 us
    ppermute x1, waiting for transfers between devices, per_device(): lax.ppermute(mine, 'shard', [(i, (i + hop) % shards) for i in range(shard...  11.2 us
    dot_general x2, matrix products, per_device(): lax.dot_general(gs[e], w_down[e], (((1,), (1,)), ((), ())), preferred_ele...  7.47 us
    unnamed x32, local copies, waits for them, and re-layouts  5.28 us
  transfers between devices with their start and end apart: 2, of which 1 were waited for; matrix products, arithmetic and copies ran while one was open for 8% of the time, Pallas kernels for 69%

profile of v2, /device:TPU:0, one launch (start us, length us, event | category | flops | bytes accessed | tf_op | source)
XLA Modules:
  0.0 256.4 jit_solution(6847386497741314404)
XLA Ops:
  8.5 3.0 %collective-permute-start = (bf16[2,128,1024]{2,1,0:T(8,128)(2,1)S(1)}, bf16[2,128,1024]{2,1,0:T(8,128)(2,1)S(1)}, u32[]{:S(2)}, u32[]{:S(2)}) collective-permute-start(bf16[2,128,1024]{2,1,0:T(8,128)(2,1)S(1)} %get-tuple-element.19), channel_id=1, source_target_pairs={{0,1},{1,0},{2,3},{3,2},{4,5},{5,4},{6,7},{7,6},{8,9},{9,8},{10,11... | collective-permute-start | bytes 1572872 | tf_op jit(solution)/shard_map/ppermute | solution.py:197
  12.2 11.2 %collective-permute-done = bf16[2,128,1024]{2,1,0:T(8,128)(2,1)S(1)} collective-permute-done((bf16[2,128,1024]{2,1,0:T(8,128)(2,1)S(1)}, bf16[2,128,1024]{2,1,0:T(8,128)(2,1)S(1)}, u32[]{:S(2)}, u32[]{:S(2)}) %collective-permute-start) | collective-permute-done | bytes 524320 | tf_op jit(solution)/shard_map/ppermute | solution.py:197
  23.7 1.3 broadcast_select_fusion.3
  25.0 3.8 %fusion.8 = f32[256,2048]{1,0:T(8,128)S(1)} fusion(bf16[2,2048,1024]{2,1,0:T(8,128)(2,1)} %param.13, bf16[1,256,1024]{2,1,0:T(8,128)(2,1)S(1)} %get-tuple-element.12), kind=kOutput, calls=%fused_computation.8 | convolution fusion | flops 1073741824 | bytes 6815744 | tf_op jit(solution)/shard_map/dot_general | solution.py:217
  28.8 3.6 %fusion.24 = f32[256,2048]{1,0:T(8,128)S(1)} fusion(f32[256,2048]{1,0:T(8,128)S(1)} %fusion.8, bf16[2,2048,1024]{2,1,0:T(8,128)(2,1)} %param.13, bf16[1,256,1024]{2,1,0:T(8,128)(2,1)S(1)} %get-tuple-element.11), kind=kOutput, calls=%fused_computation.25 | convolution fusion | flops 1074266112 | bytes 8912896 | tf_op jit(solution)/shard_map/dot_general | solution.py:217
  32.5 2.4 fusion.50
  34.9 3.3 %multiply_convert_fusion.2 = (bf16[256,2048]{1,0:T(8,128)(2,1)S(1)}, bf16[256,2048]{1,0:T(8,128)(2,1)S(1)}, bf16[256,2048]{1,0:T(8,128)(2,1)S(1)}) fusion(f32[256,2048]{1,0:T(8,128)S(1)} %fusion.50, f32[256,2048]{1,0:T(8,128)S(1)} %fusion.24, bf16[2048,2048]{1,0:T(8,128)(2,1)S(1)} %bitcast.123, bf16[256,1024]{1,0:T(8,128)(2,1)S(1)} %get-tuple-element.16, ...), kind=kOutput, calls=%fused_computation.30 | convolution fusion | flops 2157445120 | bytes 16777216 | tf_op jit(solution)/shard_map/dot_general | solution.py:215
  38.2 1.4 fusion.4
  39.7 1.4 fusion
  41.2 1.4 slice-done.1
  42.6 1.3 fusion.10
  43.9 1.3 fusion.46
  45.2 1.6 fusion.28
  46.9 1.4 fusion.37
  48.3 1.6 pad_maximum_fusion.1
  53.0 1.5 pad_maximum_fusion.3
  54.5 2.3 copy.24
  56.8 2.5 copy.23
  59.3 1.7 maximum_bitcast_fusion
  61.1 1.5 copy.25
  62.6 2.0 pad_maximum_fusion
  64.6 177.4 %shard_map.110 = f32[24,128,256]{2,1,0:T(8,128)} custom-call(bf16[24,256,256]{2,1,0:T(8,128)(2,1)} %bitcast.109, bf16[4,2,512,256]{3,2,1,0:T(8,128)(2,1)} %bitcast.112), custom_call_target="tpu_custom_call" | custom-call | flops 6442450944 | bytes 400000000 | tf_op jit(solution)/shard_map/pallas_call | solution.py:155
  242.0 2.2 slice_bitcast_fusion
  247.5 1.3 convert_element_type.31
  (48 shorter events, 9.5 us)
Async XLA Ops:
  7.2 16.5 %copy-start.7 = (f32[256]{0:T(256)S(1)}, f32[256]{0:T(256)}, u32[]{:S(2)}) copy-start(f32[256]{0:T(256)} %param.10) | copy-start | bytes 3076
  7.2 240.3 %reduce-scatter.2.cloned.1.call-start = ((), (), s32[]{:S(2)}) async-start(), calls=%async_computation.1 | async-start | bytes 3145728 | tf_op jit(solution)/shard_map/reduce_scatter | solution.py:245
  8.5 15.0 %collective-permute-start = (bf16[2,128,1024]{2,1,0:T(8,128)(2,1)S(1)}, bf16[2,128,1024]{2,1,0:T(8,128)(2,1)S(1)}, u32[]{:S(2)}, u32[]{:S(2)}) collective-permute-start(bf16[2,128,1024]{2,1,0:T(8,128)(2,1)S(1)} %get-tuple-element.19), channel_id=1, source_target_pairs={{0,1},{1,0},{2,3},{3,2},{4,5},{5,4},{6,7},{7,6},{8,9},{9,8},{10,11... | collective-permute-start | bytes 1572872 | tf_op jit(solution)/shard_map/ppermute | solution.py:197
  23.7 8.8 %slice-start.4 = ((s8[8388608]{0:T(1024)(128)(4,1)}), s8[4194304]{0:T(1024)(128)(4,1)S(1)}, s32[]{:S(2)}) async-start(s8[8388608]{0:T(1024)(128)(4,1)} %bitcast.124), calls=%async_computation.6 | async-start | bytes 8388608
  24.9 7.5 %slice-start.5 = ((s8[8388608]{0:T(1024)(128)(4,1)}), s8[4194304]{0:T(1024)(128)(4,1)S(1)}, s32[]{:S(2)}) async-start(s8[8388608]{0:T(1024)(128)(4,1)} %bitcast.124), calls=%async_computation.7 | async-start | bytes 8388608
  28.8 6.1 %slice-start.2 = ((s8[8388608]{0:T(1024)(128)(4,1)}), s8[4194304]{0:T(1024)(128)(4,1)S(1)}, s32[]{:S(2)}) async-start(s8[8388608]{0:T(1024)(128)(4,1)} %bitcast.121), calls=%async_computation.4 | async-start | bytes 8388608
  32.5 2.4 slice-start.3
  38.2 5.7 %copy-start.5 = (bf16[256,2048]{1,0:T(8,128)(2,1)}, bf16[256,2048]{1,0:T(8,128)(2,1)S(1)}, u32[]{:S(2)}) copy-start(bf16[256,2048]{1,0:T(8,128)(2,1)S(1)} %get-tuple-element.5) | copy-start | bytes 3145732
  38.2 8.6 %copy-start.3 = (bf16[256,2048]{1,0:T(8,128)(2,1)}, bf16[256,2048]{1,0:T(8,128)(2,1)S(1)}, u32[]{:S(2)}) copy-start(bf16[256,2048]{1,0:T(8,128)(2,1)S(1)} %get-tuple-element.6) | copy-start | bytes 3145732
  38.2 2.9 %slice-start = ((s8[8388608]{0:T(1024)(128)(4,1)}), s8[4194304]{0:T(1024)(128)(4,1)S(1)}, s32[]{:S(2)}) async-start(s8[8388608]{0:T(1024)(128)(4,1)} %bitcast.110), calls=%async_computation.2 | async-start | bytes 8388608
  39.6 3.0 %slice-start.1 = ((s8[8388608]{0:T(1024)(128)(4,1)}), s8[4194304]{0:T(1024)(128)(4,1)S(1)}, s32[]{:S(2)}) async-start(s8[8388608]{0:T(1024)(128)(4,1)} %bitcast.110), calls=%async_computation.3 | async-start | bytes 8388608
  48.3 1.6 copy-start.6
  50.3 1.2 copy-start.4
  50.8 2.2 copy-start.1
  50.8 2.2 copy-start.2
  61.0 1.6 copy-start
Sparse Core Ops, SparseCore 0:
  50.1 33.2 reduce-scatter.1
